TPU v7x, 32 devices: a whole 2x2x4 slice. The times are simulated.
32 devices in a mesh: batch: 8 (over y, x, core), lib: 4 (over z).
Axes of the slice: x: 2, y: 2, z: 4, core: 2. Of those that a mesh axis runs over, the one named last changes fastest.
Arguments:
- skip_features: bfloat16 [64, 1024, 320], P(('batch', 'lib')), may hold values from -6 to 6
- cached_deep_features: bfloat16 [64, 1024, 640], P('lib', 'batch'), may hold values from -6 to 6
- target_position: int32 [4, 16], P('lib'), may hold values from 0 to 15, each once within a row
- request_adapter: int32 [64], P(('batch', 'lib')), may hold values from 0 to 15
- library_adapter: int32 [16], P('lib'), may hold values from 0 to 15, each once
- adapter_down_weight: bfloat16 [16, 64, 960], P('lib'), may hold values from -0.1875 to 0.1875
- adapter_up_weight: bfloat16 [16, 64, 320], P('lib'), may hold values from -0.75 to 0.75
- kernel_weight: bfloat16 [3, 3, 960, 320], replicated, may hold values from -0.0625 to 0.0625
- shortcut_matrix: bfloat16 [960, 320], replicated, may hold values from -0.1875 to 0.1875
- group_norm_gain: float32 [960], replicated, may hold values from 0.5 to 1.5
- group_norm_offset: float32 [960], replicated, may hold values from -1.8 to 1.8
- output_bias: float32 [320], replicated, may hold values from -1.8 to 1.8
Outputs:
- block_out: bfloat16 [64, 1024, 320], P(('batch', 'lib'))
Inputs may be any that keep to these rules, and one draw needn't show every extreme that they name: Each row of target_position names every one of its 16 slots once. `request_adapter`: ids of adapters in the library. `library_adapter`: every adapter id is held in exactly one library slot.
All inputs are finite; a program needn't handle non-finite values.
Results may differ from a plain program's by a relative error of at most 0.0045.
Values may be sent and summed in bfloat16 or wider, within the bound.
A program may use at most 128 MiB of HBM per device.

v0:
```python
import jax
import jax.numpy as jnp
from jax import lax
from jax.sharding import PartitionSpec as P

DEEP = 640
GROUPS = 32
ROWS = 32
LAT_W = 32


def norm_silu(joined, group_norm_gain, group_norm_offset):
    count = joined.shape[0]
    places = joined.shape[1]
    width = joined.shape[2]
    values = joined.astype(jnp.float32).reshape(count, places, GROUPS, width // GROUPS)
    center = jnp.mean(values, axis=(1, 3), keepdims=True)
    spread = jnp.mean((values - center) ** 2, axis=(1, 3), keepdims=True)
    scaled = ((values - center) / jnp.sqrt(spread + 1e-05)).reshape(
        count, places, width
    ) * group_norm_gain + group_norm_offset
    return jax.nn.silu(scaled).astype(jnp.bfloat16)


def local(
    skip_features,
    cached_deep_features,
    target_position,
    request_adapter,
    library_adapter,
    adapter_down_weight,
    adapter_up_weight,
    kernel_weight,
    shortcut_matrix,
    group_norm_gain,
    group_norm_offset,
    output_bias,
):
    batch_count = lax.axis_size("batch")
    per_device = skip_features.shape[0]
    places = skip_features.shape[1]
    column = target_position.shape[1]
    width = kernel_weight.shape[2]
    outputs = kernel_weight.shape[3]
    placing = target_position[0]
    inverse = jnp.zeros((column,), jnp.int32).at[placing].set(jnp.arange(column, dtype=jnp.int32))
    order = inverse.reshape(batch_count, per_device).T
    outgoing = cached_deep_features[order]
    arrived = lax.all_to_all(outgoing, "batch", split_axis=1, concat_axis=1, tiled=True)
    deep = arrived.reshape(per_device, places, DEEP)
    down_portion = lax.all_gather(adapter_down_weight, "lib", axis=0, tiled=True)
    up_portion = lax.all_gather(adapter_up_weight, "lib", axis=0, tiled=True)
    id_piece = lax.all_gather(library_adapter, "lib", axis=0, tiled=True)
    picker = (request_adapter[:, None] == id_piece[None, :]).astype(jnp.bfloat16)
    down_sum = jnp.einsum("rk,kij->rij", picker, down_portion, preferred_element_type=jnp.float32)
    up_sum = jnp.einsum("rk,kij->rij", picker, up_portion, preferred_element_type=jnp.float32)
    down_sum, up_sum = (down_sum, up_sum)
    down_blocks = down_sum.astype(jnp.bfloat16)
    up_blocks = up_sum.astype(jnp.bfloat16)
    joined = jnp.concatenate([skip_features, deep], axis=2)
    normed = norm_silu(joined, group_norm_gain, group_norm_offset)
    padded = jnp.pad(
        normed.reshape(per_device, ROWS, LAT_W, width), ((0, 0), (1, 1), (1, 1), (0, 0))
    )
    conv = jnp.zeros((per_device * places, outputs), jnp.float32)
    for row_off in range(3):
        for col_off in range(3):
            window = padded[:, row_off : row_off + ROWS, col_off : col_off + LAT_W].reshape(
                per_device * places, width
            )
            conv = conv + jnp.dot(
                window, kernel_weight[row_off, col_off], preferred_element_type=jnp.float32
            )
    shortcut = jnp.dot(
        joined.reshape(per_device * places, width),
        shortcut_matrix,
        preferred_element_type=jnp.float32,
    )
    low = jnp.einsum(
        "rpc,rkc->rpk", normed, down_blocks, preferred_element_type=jnp.float32
    ).astype(jnp.bfloat16)
    delta = jnp.einsum("rpk,rko->rpo", low, up_blocks, preferred_element_type=jnp.float32)
    total = (shortcut + conv).reshape(per_device, places, outputs) + output_bias + delta
    return total.astype(jnp.bfloat16)


def solution(mesh):
    in_specs = (
        P(("batch", "lib"), None, None),
        P("lib", "batch", None),
        P("lib", None),
        P(("batch", "lib")),
        P("lib"),
        P("lib", None, None),
        P("lib", None, None),
        P(),
        P(),
        P(),
        P(),
        P(),
    )
    out_specs = P(("batch", "lib"), None, None)
    return jax.shard_map(local, mesh=mesh, in_specs=in_specs, out_specs=out_specs, check_vma=False)
```

profile of v0, /device:TPU:0, one launch (start us, length us, event | category | flops | bytes accessed | tf_op | source)
XLA Modules:
  0.0 148.1 jit_solution(5434966734072437644)
XLA Ops:
  6.5 0.8 fusion.48
  7.3 0.6 scatter_custom_fusion
  8.0 0.1 reshape.168
  8.1 0.1 copy.33
  8.1 0.1 reshape.181
  8.2 0.1 copy-done
  8.3 2.4 %gather_fusion = bf16[16,128,640]{2,1,0:T(8,128)(2,1)} fusion(bf16[16,128,640]{2,1,0:T(8,128)(2,1)S(1)} %copy-done, s32[1024]{0:T(1024)S(1)} %pad_clamp_fusion), kind=kCustom, calls=%fused_computation | custom fusion | bytes 5242944 | tf_op jit(solution)/shard_map/gather | solution.py:48
  10.7 3.6 %copy.34 = bf16[2,8,128,640]{3,2,0,1:T(8,128)(2,1)} copy(bf16[2,8,128,640]{3,2,1,0:T(8,128)(2,1)} %bitcast.86) | data formatting | bytes 5242880 | tf_op jit(solution)/shard_map/gather | solution.py:48
  14.3 5.3 %all-to-all-start = ((bf16[2,8,128,640]{3,2,0,1:T(8,128)(2,1)}), bf16[2,8,128,640]{3,2,0,1:T(8,128)(2,1)}, u32[]{:S(2)}, u32[]{:S(2)}) async-start(bf16[2,8,128,640]{3,2,0,1:T(8,128)(2,1)} %copy.34), calls=%async_computation | async-start | bytes 5242880 | tf_op jit(solution)/shard_map/all_to_all | solution.py:49
  19.6 0.0 all-gather.2.cloned.1.call-start
  19.6 0.7 all-gather.2.cloned.1.call-update
  20.3 1.6 %copy.49 = bf16[2,1024,320]{2,1,0:T(8,128)(2,1)} copy(bf16[2,1024,320]{1,2,0:T(8,128)(2,1)S(1)} %copy-done.9) | data formatting | bytes 2621440 | tf_op jit(solution)/shard_map/concatenate | solution.py:60
  21.9 0.6 dynamic-slice
  23.2 0.2 dynamic-update-slice
  23.4 9.2 %all-reduce.1 = s32[16]{0:T(128)S(1)} all-reduce(s32[16]{0:T(128)S(1)} %dynamic-update-slice), channel_id=1, replica_groups=mesh['batch'=8,'lib'=4] {'lib'}, use_global_device_ids=true, to_apply=%add.1 | all-reduce | flops 16 | bytes 128
  32.6 29.5 %all_gather.11 = bf16[16,64,320]{2,1,0:T(8,128)(2,1)S(1)} all-gather(bf16[4,64,320]{2,1,0:T(8,128)(2,1)S(1)} %copy-done.10), channel_id=1, replica_groups=mesh['batch'=8,'lib'=4] {'lib'}, dimensions={0}, use_global_device_ids=true | all-gather | bytes 819200 | tf_op jit(solution)/shard_map/all_gather | solution.py:52
  62.1 0.5 convolution_convert_fusion.1
  62.7 2.2 %copy.35 = bf16[2,8,128,640]{3,2,1,0:T(8,128)(2,1)S(1)} copy(bf16[2,8,128,640]{3,2,0,1:T(8,128)(2,1)} %all-to-all-done) | data formatting | bytes 5242880 | tf_op jit(solution)/shard_map/all_to_all | solution.py:49
  64.9 1.7 %convert_reduce_fusion = f32[2,960]{1,0:T(2,128)S(1)} fusion(bf16[2,1024,640]{2,1,0:T(8,128)(2,1)S(1)} %bitcast.72, bf16[2,1024,320]{2,1,0:T(8,128)(2,1)S(1)} %copy-done.2), kind=kLoop, calls=%fused_computation.3 | loop fusion | flops 9828480 | bytes 3939840 | tf_op jit(solution)/shard_map/reduce_sum | solution.py:17
  66.7 0.1 reduce_sum.24
  66.8 0.1 reduce_sum.25
  66.9 0.1 sub.31
  66.9 0.1 sub.32
  67.1 3.6 %fusion.2 = f32[2,960]{1,0:T(2,128)S(1)} fusion(f32[2,960]{1,0:T(2,128)S(1)} %sub.32, bf16[2,1024,640]{2,1,0:T(8,128)(2,1)S(1)} %bitcast.73, bf16[2,1024,320]{2,1,0:T(8,128)(2,1)} %copy.49), kind=kLoop, calls=%fused_computation.6 | loop fusion | flops 13760640 | bytes 3947520 | tf_op jit(solution)/shard_map/reduce_sum | solution.py:18
  70.7 0.1 reduce_sum.36
  70.8 0.1 reduce_sum.37
  70.9 0.1 div.49
  70.9 0.1 div.50
  71.1 6.8 %multiply_convert_fusion = bf16[2,1024,960]{2,1,0:T(8,128)(2,1)} fusion(f32[960]{0:T(1024)S(1)} %copy-done.11, f32[960]{0:T(1024)S(1)} %copy-done.12, f32[2,960]{1,0:T(2,128)S(1)} %div.50, f32[2,960]{1,0:T(2,128)S(1)} %sub.32, bf16[2,1024,640]{2,1,0:T(8,128)(2,1)S(1)} %bitcast.74, bf16[2,1024,320]{2,1,0:T(8,128)(2,1)} %copy.49), kind=kLoop, calls=%fused_computation.9 | loop fusion | flops 25559040 | bytes 7887360 | tf_op jit(solution)/shard_map/convert_element_type | solution.py:22
  77.9 5.6 %multiply_convert_fusion.1 = bf16[2,32,32,960]{3,2,1,0:T(8,128)(2,1)} fusion(bf16[2,32,32,640]{3,2,1,0:T(8,128)(2,1)S(1)} %bitcast.75, bf16[2,32,32,320]{3,2,1,0:T(8,128)(2,1)S(1)} %bitcast.77, f32[960]{0:T(1024)S(1)} %copy-done.11, f32[960]{0:T(1024)S(1)} %copy-done.12, f32[2,960]{1,0:T(2,128)S(1)} %div.50, f32[2,960]{1,0:T(2,128)S(1)} %sub.32), kind=kLoop, calls=%fused_computation.10 | loop fusion | flops 25559040 | bytes 7887360 | tf_op jit(solution)/shard_map/convert_element_type | solution.py:22
  83.5 22.2 %pad_slice_fusion = (bf16[2,32,32,960]{3,2,1,0:T(8,128)(2,1)S(1)}, bf16[2,32,32,960]{3,2,1,0:T(8,128)(2,1)}, bf16[2,32,32,960]{3,2,1,0:T(8,128)(2,1)}, bf16[2,32...) fusion(bf16[2,32,32,960]{3,2,1,0:T(8,128)(2,1)} %multiply_conve, ...), kind=kLoop, calls=%fused_computation.11 | loop fusion | bytes 35389440 | tf_op jit(solution)/shard_map/slice | solution.py:68
  105.8 0.0 slice-start
  105.8 4.1 %fusion.30 = f32[2048,320]{0,1:T(8,128)S(1)} fusion(bf16[2048,960]{1,0:T(8,128)(2,1)} %bitcast.88, bf16[3,3,960,320]{2,3,1,0:T(8,128)(2,1)} %param.19), kind=kOutput, calls=%fused_computation.51 | convolution fusion | flops 1258291200 | bytes 7471104 | tf_op jit(solution)/shard_map/dot_general | solution.py:71
  109.9 0.0 slice-start.1
  109.9 2.8 %convolution_add_fusion.6 = f32[2048,320]{0,1:T(8,128)S(1)} fusion(f32[2048,320]{0,1:T(8,128)S(1)} %fusion.30, bf16[2048,960]{1,0:T(8,128)(2,1)S(1)} %bitcast.84, bf16[3,3,960,320]{2,3,1,0:T(8,128)(2,1)} %param.19), kind=kOutput, calls=%fused_computation.32 | convolution fusion | flops 1258946560 | bytes 9830400 | tf_op jit(solution)/shard_map/dot_general | solution.py:71
  112.7 0.2 slice-done.1
  112.9 1.6 %convolution_add_fusion.5 = f32[2048,320]{0,1:T(8,128)S(1)} fusion(f32[2048,320]{0,1:T(8,128)S(1)} %convolution_add_fusion.6, bf16[2048,960]{1,0:T(8,128)(2,1)S(1)} %bitcast.83, bf16[3,3,960,320]{2,3,1,0:T(8,128)(2,1)S(1)} %bitcast.90), kind=kOutput, calls=%fused_computation.31 | convolution fusion | flops 1258946560 | bytes 10092544 | tf_op jit(solution)/shard_map/dot_general | solution.py:71
  114.5 0.6 copy-done.4
  115.1 1.6 %convolution_add_fusion.4 = f32[2048,320]{0,1:T(8,128)S(1)} fusion(f32[2048,320]{0,1:T(8,128)S(1)} %convolution_add_fusion.5, bf16[2048,960]{1,0:T(8,128)(2,1)S(1)} %bitcast.82, bf16[3,3,960,320]{2,3,1,0:T(8,128)(2,1)S(1)} %bitcast.90), kind=kOutput, calls=%fused_computation.30 | convolution fusion | flops 1258946560 | bytes 10092544 | tf_op jit(solution)/shard_map/dot_general | solution.py:71
  116.7 0.6 copy-done.8
  117.3 3.1 %fusion.24 = f32[2048,320]{0,1:T(8,128)} fusion(bf16[2048,960]{1,0:T(8,128)(2,1)S(1)} %bitcast.87, bf16[3,3,960,320]{2,3,1,0:T(8,128)(2,1)S(1)} %bitcast.90), kind=kOutput, calls=%fused_computation.45 | convolution fusion | flops 1258291200 | bytes 7471104 | tf_op jit(solution)/shard_map/dot_general | solution.py:71
  120.4 3.5 %fusion.12 = f32[2048,320]{0,1:T(8,128)S(1)} fusion(f32[2048,320]{0,1:T(8,128)} %fusion.24, f32[2048,320]{0,1:T(8,128)S(1)} %convolution_add_fusion.4, bf16[2048,960]{1,0:T(8,128)(2,1)S(1)} %bitcast.85, bf16[3,3,960,320]{2,3,1,0:T(8,128)(2,1)S(1)} %bitcast.90), kind=kOutput, calls=%fused_computation.26 | convolution fusion | flops 1259601920 | bytes 12713984 | tf_op jit(solution)/shard_map/dot_general | solution.py:71
  123.9 1.6 %convolution_add_fusion.3 = f32[2048,320]{0,1:T(8,128)S(1)} fusion(f32[2048,320]{0,1:T(8,128)S(1)} %fusion.12, bf16[2048,960]{1,0:T(8,128)(2,1)S(1)} %bitcast.81, bf16[3,3,960,320]{2,3,1,0:T(8,128)(2,1)S(1)} %bitcast.90), kind=kOutput, calls=%fused_computation.29 | convolution fusion | flops 1258946560 | bytes 10092544 | tf_op jit(solution)/shard_map/dot_general | solution.py:71
  125.5 1.6 %convolution_add_fusion.2 = f32[2048,320]{0,1:T(8,128)S(1)} fusion(f32[2048,320]{0,1:T(8,128)S(1)} %convolution_add_fusion.3, bf16[2048,960]{1,0:T(8,128)(2,1)S(1)} %bitcast.80, bf16[3,3,960,320]{2,3,1,0:T(8,128)(2,1)S(1)} %bitcast.90), kind=kOutput, calls=%fused_computation.28 | convolution fusion | flops 1258946560 | bytes 10092544 | tf_op jit(solution)/shard_map/dot_general | solution.py:71
  127.2 1.9 %convolution_add_fusion.1 = f32[2048,320]{0,1:T(8,128)S(1)} fusion(f32[2048,320]{0,1:T(8,128)S(1)} %convolution_add_fusion.2, bf16[2048,960]{1,0:T(8,128)(2,1)S(1)} %bitcast.79, bf16[3,3,960,320]{2,3,1,0:T(8,128)(2,1)S(1)} %bitcast.90), kind=kOutput, calls=%fused_computation.27 | convolution fusion | flops 1258946560 | bytes 10092544 | tf_op jit(solution)/shard_map/dot_general | solution.py:71
  129.1 3.3 %fusion.9 = f32[2048,320]{0,1:T(8,128)} fusion(f32[2048,320]{0,1:T(8,128)S(1)} %convolution_add_fusion.1, bf16[960,320]{0,1:T(8,128)(2,1)S(1)} %copy-done.15, bf16[2048,640]{1,0:T(8,128)(2,1)S(1)} %bitcast.76, bf16[2048,320]{1,0:T(8,128)(2,1)S(1)} %bitcast.78), kind=kOutput, calls=%fused_computation.24 | convolution fusion | flops 1266810880 | bytes 9789440 | tf_op jit(solution)/shard_map/dot_general | solution.py:74
  132.4 2.9 %fusion.17 = bf16[2,64,960]{2,0,1:T(2,128)(2,1)S(1)} fusion(bf16[16,64,960]{2,1,0:T(8,128)(2,1)} %all-gather.2.cloned.1.call-done, s32[16]{0:T(128)S(1)} %all-reduce.1, s32[2]{0:T(128)S(1)} %copy-done.14), kind=kOutput, calls=%fused_computation.39 | convolution fusion | flops 4055072 | bytes 2211912 | tf_op jit(solution)/shard_map/rk,kij->rij/dot_general | solution.py:55
  135.3 6.0 %fusion.14 = bf16[2,1024,320]{1,2,0:T(8,128)(2,1)} fusion(f32[40,2,8,1024]{3,2,1,0:T(8,128)} %bitcast.91, f32[320]{0:T(512)S(1)} %copy-done.13, bf16[2,1024,960]{2,1,0:T(8,128)(2,1)} %multiply_convert_fusion, bf16[2,64,960]{2,0,1:T(2,128)(2,1)S(1)} %fusion.17, bf16[2,64,320]{2,0,1:T(2,128)(2,1)S(1)} %convolution_convert_fusion.1), kind=kOutput, calls=%fused_computation.35 | convolution fusion | flops 337641472 | bytes 8193280 | tf_op jit(solution)/shard_map/rpk,rko->rpo/dot_general | solution.py:82
  (43 shorter events, 0.1 us)
Async XLA Ops:
  6.5 1.8 %copy-start = (bf16[16,128,640]{2,1,0:T(8,128)(2,1)S(1)}, bf16[16,128,640]{2,1,0:T(8,128)(2,1)}, u32[]{:S(2)}) copy-start(bf16[16,128,640]{2,1,0:T(8,128)(2,1)} %param.13) | copy-start | bytes 7864324
  14.3 6.1 %copy-start.9 = (bf16[2,1024,320]{1,2,0:T(8,128)(2,1)S(1)}, bf16[2,1024,320]{1,2,0:T(8,128)(2,1)}, u32[]{:S(2)}) copy-start(bf16[2,1024,320]{1,2,0:T(8,128)(2,1)} %param.12) | copy-start | bytes 3932164
  14.3 7.7 %copy-start.17 = (u32[32]{0:T(128)S(1)}, u32[32]{0:T(128)}, u32[]{:S(2)}) copy-start(u32[32]{0:T(128)} %constant.27) | copy-start | bytes 388
  14.3 8.9 %copy-start.16 = (s32[4]{0:T(128)S(1)}, s32[4]{0:T(128)}, u32[]{:S(2)}) copy-start(s32[4]{0:T(128)} %param.16) | copy-start | bytes 52
  14.3 18.3 %copy-start.10 = (bf16[4,64,320]{2,1,0:T(8,128)(2,1)S(1)}, bf16[4,64,320]{2,1,0:T(8,128)(2,1)}, u32[]{:S(2)}) copy-start(bf16[4,64,320]{2,1,0:T(8,128)(2,1)} %param.18) | copy-start | bytes 491524
  14.3 47.8 %copy-start.14 = (s32[2]{0:T(128)S(1)}, s32[2]{0:T(128)}, u32[]{:S(2)}) copy-start(s32[2]{0:T(128)} %param.15) | copy-start | bytes 28
  14.3 48.4 %all-to-all-start = ((bf16[2,8,128,640]{3,2,0,1:T(8,128)(2,1)}), bf16[2,8,128,640]{3,2,0,1:T(8,128)(2,1)}, u32[]{:S(2)}, u32[]{:S(2)}) async-start(bf16[2,8,128,640]{3,2,0,1:T(8,128)(2,1)} %copy.34), calls=%async_computation | async-start | bytes 5242880 | tf_op jit(solution)/shard_map/all_to_all | solution.py:49
  19.6 112.8 %all-gather.2.cloned.1.call-start = ((), (), s32[]{:S(2)}) async-start(), calls=%async_computation.1 | async-start | bytes 2621440 | tf_op jit(solution)/shard_map/all_gather | solution.py:51
  62.7 2.2 %copy-start.2 = (bf16[2,1024,320]{2,1,0:T(8,128)(2,1)S(1)}, bf16[2,1024,320]{2,1,0:T(8,128)(2,1)}, u32[]{:S(2)}) copy-start(bf16[2,1024,320]{2,1,0:T(8,128)(2,1)} %copy.49) | copy-start | bytes 3932164
  64.9 6.2 %copy-start.11 = (f32[960]{0:T(1024)S(1)}, f32[960]{0:T(1024)}, u32[]{:S(2)}) copy-start(f32[960]{0:T(1024)} %param.22) | copy-start | bytes 11524
  64.9 6.2 %copy-start.12 = (f32[960]{0:T(1024)S(1)}, f32[960]{0:T(1024)}, u32[]{:S(2)}) copy-start(f32[960]{0:T(1024)} %param.21) | copy-start | bytes 11524
  71.1 6.9 %copy-start.3 = (bf16[2,1024,320]{2,1,0:T(8,128)(2,1)S(1)}, bf16[2,1024,320]{2,1,0:T(8,128)(2,1)}, u32[]{:S(2)}) copy-start(bf16[2,1024,320]{2,1,0:T(8,128)(2,1)} %copy.49) | copy-start | bytes 3932164
  105.8 4.1 %copy-start.6 = (bf16[2,32,32,960]{3,2,1,0:T(8,128)(2,1)S(1)}, bf16[2,32,32,960]{3,2,1,0:T(8,128)(2,1)}, u32[]{:S(2)}) copy-start(bf16[2,32,32,960]{3,2,1,0:T(8,128)(2,1)} %get-tuple-element.6) | copy-start | bytes 11796484
  105.8 6.9 %slice-start = ((s8[5898240]{0:T(1024)(128)(4,1)}), s8[4194304]{0:T(1024)(128)(4,1)S(1)}, s32[]{:S(2)}) async-start(s8[5898240]{0:T(1024)(128)(4,1)} %bitcast.89), calls=%async_computation.2 | async-start | bytes 8388608
  109.9 2.9 %copy-start.5 = (bf16[2,32,32,960]{3,2,1,0:T(8,128)(2,1)S(1)}, bf16[2,32,32,960]{3,2,1,0:T(8,128)(2,1)}, u32[]{:S(2)}) copy-start(bf16[2,32,32,960]{3,2,1,0:T(8,128)(2,1)} %get-tuple-element.7) | copy-start | bytes 11796484
  109.9 3.0 %slice-start.1 = ((s8[5898240]{0:T(1024)(128)(4,1)}), s8[1703936]{0:T(1024)(128)(4,1)S(1)}, s32[]{:S(2)}) async-start(s8[5898240]{0:T(1024)(128)(4,1)} %bitcast.89), calls=%async_computation.3 | async-start | bytes 3407872
  112.9 2.2 %copy-start.4 = (bf16[2,32,32,960]{3,2,1,0:T(8,128)(2,1)S(1)}, bf16[2,32,32,960]{3,2,1,0:T(8,128)(2,1)}, u32[]{:S(2)}) copy-start(bf16[2,32,32,960]{3,2,1,0:T(8,128)(2,1)} %get-tuple-element.8) | copy-start | bytes 11796484
  115.1 2.2 %copy-start.8 = (bf16[2,32,32,960]{3,2,1,0:T(8,128)(2,1)S(1)}, bf16[2,32,32,960]{3,2,1,0:T(8,128)(2,1)}, u32[]{:S(2)}) copy-start(bf16[2,32,32,960]{3,2,1,0:T(8,128)(2,1)} %get-tuple-element.9) | copy-start | bytes 11796484
  117.3 3.1 %copy-start.7 = (bf16[2,1024,960]{2,1,0:T(8,128)(2,1)S(1)}, bf16[2,1024,960]{2,1,0:T(8,128)(2,1)}, u32[]{:S(2)}) copy-start(bf16[2,1024,960]{2,1,0:T(8,128)(2,1)} %multiply_convert_fusion) | copy-start | bytes 11796484
  127.2 1.9 %copy-start.15 = (bf16[960,320]{0,1:T(8,128)(2,1)S(1)}, bf16[960,320]{0,1:T(8,128)(2,1)}, u32[]{:S(2)}) copy-start(bf16[960,320]{0,1:T(8,128)(2,1)} %param.20) | copy-start | bytes 1843204
  129.1 6.2 %copy-start.13 = (f32[320]{0:T(512)S(1)}, f32[320]{0:T(512)}, u32[]{:S(2)}) copy-start(f32[320]{0:T(512)} %param.23) | copy-start | bytes 3844
  135.3 6.0 %copy-start.1 = (bf16[16,128,640]{2,1,0:T(8,128)(2,1)S(1)}, bf16[16,128,640]{2,1,0:T(8,128)(2,1)}, u32[]{:S(2)}) copy-start(bf16[16,128,640]{2,1,0:T(8,128)(2,1)} %param.13) | copy-start | bytes 7864324
Sparse Core Ops, SparseCore 0:
  22.0 60.5 all-gather.1
where the time goes:
time: 149 us; the launch traced here: 148 us
  blocking collectives  38.7 us (26%)
  local copies, waits for them, and re-layouts  35.9 us (24%)
  matrix products  34.4 us (23%)
  other arithmetic  18.8 us (13%)
  between operations  14.4 us (10%)
  starting transfers between devices  5.35 us (4%)
    all_gather x1, blocking collectives, local(): up_portion = lax.all_gather(adapter_up_weight, 'lib', axis=0, tiled=True)  29.5 us
    slice x1, local copies, waits for them, and re-layouts, local(): padded[:, row_off:row_off + ROWS, col_off:col_off + LAT_W]  22.2 us
    dot_general x9, matrix products, local(): jnp.dot(window, kernel_weight[row_off, col_off], preferred_element_type=j...  21.7 us
    convert_element_type x2, other arithmetic, norm_silu(): return jax.nn.silu(scaled).astype(jnp.bfloat16)  12.4 us
    unnamed x1, blocking collectives  9.15 us
    dot_general x1, matrix products, local(): jnp.einsum('rpk,rko->rpo', low, up_blocks, preferred_element_type=jnp.flo...  5.97 us
    gather x2, local copies, waits for them, and re-layouts, local(): outgoing = cached_deep_features[order]  5.97 us
    all_to_all x1, starting transfers between devices, local(): lax.all_to_all(outgoing, 'batch', split_axis=1, concat_axis=1, tiled=True)  5.31 us
  transfers between devices with their start and end apart: 2, of which 0 were waited for; matrix products, arithmetic and copies ran while one was open for 48% of the time, Pallas kernels for 0%

commit v1 on v0

--- a/solution.py
+++ b/solution.py
@@ -1,3 +1,4 @@
+import functools
 import jax
 import jax.numpy as jnp
 from jax import lax
@@ -7,6 +8,22 @@
 GROUPS = 32
 ROWS = 32
 LAT_W = 32
+
+
+def _get_outputs(t0, mesh_dim, array_axis):
+    n_parts = lax.psum(1, mesh_dim)
+    part_next = [None] * n_parts
+    part_next[n_parts - 1] = t0
+    in_order = [(num, (num + 1) % n_parts) for num in range(n_parts)]
+    for dev in range(n_parts - 2, -1, -1):
+        part_next[dev] = lax.ppermute(part_next[dev + 1], mesh_dim, in_order)
+    answer = jnp.concatenate(part_next, array_axis)
+    g_now = lax.axis_index(mesh_dim)
+    heard = (g_now + 1) * t0.shape[array_axis]
+    return jnp.roll(answer, heard, array_axis)
+
+
+_pack_outputs = functools.partial(_get_outputs, mesh_dim="lib", array_axis=0)
 
 
 def norm_silu(joined, group_norm_gain, group_norm_offset):
@@ -49,7 +66,7 @@
     arrived = lax.all_to_all(outgoing, "batch", split_axis=1, concat_axis=1, tiled=True)
     deep = arrived.reshape(per_device, places, DEEP)
     down_portion = lax.all_gather(adapter_down_weight, "lib", axis=0, tiled=True)
-    up_portion = lax.all_gather(adapter_up_weight, "lib", axis=0, tiled=True)
+    up_portion = _pack_outputs(adapter_up_weight)
     id_piece = lax.all_gather(library_adapter, "lib", axis=0, tiled=True)
     picker = (request_adapter[:, None] == id_piece[None, :]).astype(jnp.bfloat16)
     down_sum = jnp.einsum("rk,kij->rij", picker, down_portion, preferred_element_type=jnp.float32)

time: 149 us -> 140 us (0.940)
  blocking collectives: 38.7 us -> 8.23 us
  waiting for transfers between devices: 0.68 us -> 16.1 us
  starting transfers between devices: 5.35 us -> 7.68 us
  local copies, waits for them, and re-layouts: 35.9 us -> 38.2 us
  other arithmetic: 18.8 us -> 20.5 us
    all_gather x1 -> x0, blocking collectives: 29.5 us -> none  [local(): up_portion = lax.all_gather(adapter_up_weight, 'lib', axis=0, tiled=True)]
    ppermute x0 -> x3, waiting for transfers between devices: none -> 15.8 us  [_get_outputs(): part_next[dev] = lax.ppermute(part_next[dev + 1], mesh_dim, in_order)]
    ppermute x0 -> x3, starting transfers between devices: none -> 2.34 us  [_get_outputs(): part_next[dev] = lax.ppermute(part_next[dev + 1], mesh_dim, in_order)]
    concatenate x0 -> x1, local copies, waits for them, and re-layouts: none -> 1.96 us  [_get_outputs(): return jnp.roll(answer, heard, array_axis)]
    reduce_sum x2, other arithmetic: 1.82 us -> 3.5 us  [norm_silu(): center = jnp.mean(values, axis=(1, 3), keepdims=True)]
  transfers between devices with their start and end apart: 2 -> 5, of which waited for: 0 -> 3; matrix products, arithmetic and copies ran while one was open for 48% -> 54% of each run, Pallas kernels for 0% -> 0%
where the time goes in v1:
time: 140 us; the launch traced here: 139 us
  local copies, waits for them, and re-layouts  38.2 us (27%)
  matrix products  34.2 us (24%)
  other arithmetic  20.5 us (15%)
  waiting for transfers between devices  16.1 us (12%)
  between operations  14.4 us (10%)
  blocking collectives  8.23 us (6%)
  starting transfers between devices  7.68 us (5%)
    slice x1, local copies, waits for them, and re-layouts, local(): padded[:, row_off:row_off + ROWS, col_off:col_off + LAT_W]  22.5 us
    dot_general x9, matrix products, local(): jnp.dot(window, kernel_weight[row_off, col_off], preferred_element_type=j...  21.7 us
    ppermute x3, waiting for transfers between devices, _get_outputs(): part_next[dev] = lax.ppermute(part_next[dev + 1], mesh_dim, in_order)  15.8 us
    convert_element_type x2, other arithmetic, norm_silu(): return jax.nn.silu(scaled).astype(jnp.bfloat16)  12.4 us
    unnamed x1, blocking collectives  8.23 us
    gather x2, local copies, waits for them, and re-layouts, local(): outgoing = cached_deep_features[order]  6.01 us
    dot_general x1, matrix products, local(): jnp.einsum('rpk,rko->rpo', low, up_blocks, preferred_element_type=jnp.flo...  5.96 us
    all_to_all x1, starting transfers between devices, local(): lax.all_to_all(outgoing, 'batch', split_axis=1, concat_axis=1, tiled=True)  5.3 us
  transfers between devices with their start and end apart: 5, of which 3 were waited for; matrix products, arithmetic and copies ran while one was open for 54% of the time, Pallas kernels for 0%

profile of v1, /device:TPU:0, one launch (start us, length us, event | category | flops | bytes accessed | tf_op | source)
XLA Modules:
  0.0 139.2 jit_solution(11728696801594866323)
XLA Ops:
  6.5 0.8 fusion.48
  7.3 0.6 scatter_custom_fusion
  8.0 0.1 reshape.168
  8.1 0.1 copy.35
  8.1 0.1 reshape.181
  8.3 2.4 %gather_fusion = bf16[16,128,640]{2,1,0:T(8,128)(2,1)} fusion(bf16[16,128,640]{2,1,0:T(8,128)(2,1)S(1)} %copy-done, s32[1024]{0:T(1024)S(1)} %pad_clamp_fusion), kind=kCustom, calls=%fused_computation | custom fusion | bytes 5242944 | tf_op jit(solution)/shard_map/gather | solution.py:65
  10.7 3.6 %copy.36 = bf16[2,8,128,640]{3,2,0,1:T(8,128)(2,1)} copy(bf16[2,8,128,640]{3,2,1,0:T(8,128)(2,1)} %bitcast.86) | data formatting | bytes 5242880 | tf_op jit(solution)/shard_map/gather | solution.py:65
  14.3 5.3 %all-to-all-start = ((bf16[2,8,128,640]{3,2,0,1:T(8,128)(2,1)}), bf16[2,8,128,640]{3,2,0,1:T(8,128)(2,1)}, u32[]{:S(2)}, u32[]{:S(2)}) async-start(bf16[2,8,128,640]{3,2,0,1:T(8,128)(2,1)} %copy.36), calls=%async_computation | async-start | bytes 5242880 | tf_op jit(solution)/shard_map/all_to_all | solution.py:66
  19.7 0.2 copy.48
  19.8 2.3 %collective-permute-start = (bf16[4,64,320]{2,0,1:T(4,128)(2,1)S(1)}, bf16[4,64,320]{2,0,1:T(4,128)(2,1)S(1)}, u32[]{:S(2)}, u32[]{:S(2)}) collective-permute-start(bf16[4,64,320]{2,0,1:T(4,128)(2,1)S(1)} %copy.48), channel_id=1, source_target_pairs={{0,1},{1,2},{2,3},{3,0},{4,5},{5,6},{6,7},{7,4},{8,9},{9,10},{10,1... | collective-permute-start | bytes 491528 | tf_op jit(solution)/shard_map/ppermute | solution.py:19
  22.2 7.4 %collective-permute-done = bf16[4,64,320]{2,0,1:T(4,128)(2,1)S(1)} collective-permute-done((bf16[4,64,320]{2,0,1:T(4,128)(2,1)S(1)}, bf16[4,64,320]{2,0,1:T(4,128)(2,1)S(1)}, u32[]{:S(2)}, u32[]{:S(2)}) %collective-permute-start) | collective-permute-done | bytes 163872 | tf_op jit(solution)/shard_map/ppermute | solution.py:19
  29.6 8.4 %collective-permute-done.1 = bf16[4,64,320]{2,0,1:T(4,128)(2,1)S(1)} collective-permute-done((bf16[4,64,320]{2,0,1:T(4,128)(2,1)S(1)}, bf16[4,64,320]{2,0,1:T(4,128)(2,1)S(1)}, u32[]{:S(2)}, u32[]{:S(2)}) %collective-permute-start.1) | collective-permute-done | bytes 163872 | tf_op jit(solution)/shard_map/ppermute | solution.py:19
  38.1 1.6 %copy.53 = bf16[2,1024,320]{2,1,0:T(8,128)(2,1)} copy(bf16[2,1024,320]{1,2,0:T(8,128)(2,1)S(1)} %copy-done.8) | data formatting | bytes 2621440 | tf_op jit(solution)/shard_map/concatenate | solution.py:77
  39.7 0.6 dynamic-slice
  40.9 0.2 dynamic-update-slice
  41.2 8.2 %all-reduce.1 = s32[16]{0:T(128)S(1)} all-reduce(s32[16]{0:T(128)S(1)} %dynamic-update-slice), channel_id=1, replica_groups=mesh['batch'=8,'lib'=4] {'lib'}, use_global_device_ids=true, to_apply=%add.1 | all-reduce | flops 16 | bytes 128
  49.4 2.0 %concatenate.38 = bf16[32,64,320]{2,0,1:T(8,128)(2,1)S(1)} concatenate(bf16[4,64,320]{2,0,1:T(4,128)(2,1)S(1)} %collective-permute-done.2, bf16[4,64,320]{2,0,1:T(4,128)(2,1)S(1)} %collective-permute-done.1, bf16[4,64,320]{2,0,1:T(4,128)(2,1)S(1)} %collective-permute-done, bf16[4,64,320]{2,0,1:T(4,128)(2,1)S(1)} %copy.48, bf16[4,64,320]{2,0,1:T(4,128)(2,1)S(1)} %collective-permute-done.2, ...), dimensions={0} | concatenate | bytes 2621440 | tf_op jit(solution)/shard_map/jit(_roll_dynamic)/concatenate | solution.py:23
  51.4 0.4 convolution_convert_fusion.1
  51.7 0.2 all-to-all-done
  52.0 2.1 %copy.37 = bf16[2,8,128,640]{3,2,1,0:T(8,128)(2,1)S(1)} copy(bf16[2,8,128,640]{3,2,0,1:T(8,128)(2,1)} %all-to-all-done) | data formatting | bytes 5242880 | tf_op jit(solution)/shard_map/all_to_all | solution.py:66
  54.1 3.4 %convert_reduce_fusion = f32[2,960]{1,0:T(2,128)S(1)} fusion(bf16[2,1024,640]{2,1,0:T(8,128)(2,1)S(1)} %bitcast.72, bf16[2,1024,320]{2,1,0:T(8,128)(2,1)} %copy.53), kind=kLoop, calls=%fused_computation.3 | loop fusion | flops 9828480 | bytes 3939840 | tf_op jit(solution)/shard_map/reduce_sum | solution.py:34
  57.5 0.1 reduce_sum.24
  57.6 0.1 reduce_sum.25
  57.7 0.1 sub.35
  57.8 0.1 sub.36
  57.9 3.6 %fusion.2 = f32[2,960]{1,0:T(2,128)S(1)} fusion(f32[2,960]{1,0:T(2,128)S(1)} %sub.36, bf16[2,1024,640]{2,1,0:T(8,128)(2,1)S(1)} %bitcast.73, bf16[2,1024,320]{2,1,0:T(8,128)(2,1)} %copy.53), kind=kLoop, calls=%fused_computation.6 | loop fusion | flops 13760640 | bytes 3947520 | tf_op jit(solution)/shard_map/reduce_sum | solution.py:35
  61.5 0.1 reduce_sum.36
  61.6 0.1 reduce_sum.37
  61.7 0.1 div.49
  61.8 0.1 div.50
  61.9 6.8 %multiply_convert_fusion = bf16[2,1024,960]{2,1,0:T(8,128)(2,1)} fusion(f32[960]{0:T(1024)S(1)} %copy-done.10, f32[960]{0:T(1024)S(1)} %copy-done.11, f32[2,960]{1,0:T(2,128)S(1)} %div.50, f32[2,960]{1,0:T(2,128)S(1)} %sub.36, bf16[2,1024,640]{2,1,0:T(8,128)(2,1)S(1)} %bitcast.74, bf16[2,1024,320]{2,1,0:T(8,128)(2,1)} %copy.53), kind=kLoop, calls=%fused_computation.9 | loop fusion | flops 25559040 | bytes 7887360 | tf_op jit(solution)/shard_map/convert_element_type | solution.py:39
  68.8 5.6 %multiply_convert_fusion.1 = bf16[2,32,32,960]{3,2,1,0:T(8,128)(2,1)} fusion(bf16[2,32,32,640]{3,2,1,0:T(8,128)(2,1)S(1)} %bitcast.75, bf16[2,32,32,320]{3,2,1,0:T(8,128)(2,1)S(1)} %bitcast.77, f32[960]{0:T(1024)S(1)} %copy-done.10, f32[960]{0:T(1024)S(1)} %copy-done.11, f32[2,960]{1,0:T(2,128)S(1)} %div.50, f32[2,960]{1,0:T(2,128)S(1)} %sub.36), kind=kLoop, calls=%fused_computation.10 | loop fusion | flops 25559040 | bytes 7887360 | tf_op jit(solution)/shard_map/convert_element_type | solution.py:39
  74.4 22.5 %pad_slice_fusion = (bf16[2,32,32,960]{3,2,1,0:T(8,128)(2,1)S(1)}, bf16[2,32,32,960]{3,2,1,0:T(8,128)(2,1)}, bf16[2,32,32,960]{3,2,1,0:T(8,128)(2,1)}, bf16[2,32...) fusion(bf16[2,32,32,960]{3,2,1,0:T(8,128)(2,1)} %multiply_conve, ...), kind=kLoop, calls=%fused_computation.11 | loop fusion | bytes 35389440 | tf_op jit(solution)/shard_map/slice | solution.py:85
  96.9 4.0 %fusion.30 = f32[2048,320]{0,1:T(8,128)S(1)} fusion(bf16[2048,960]{1,0:T(8,128)(2,1)} %bitcast.88, bf16[3,3,960,320]{2,3,1,0:T(8,128)(2,1)} %param.19), kind=kOutput, calls=%fused_computation.51 | convolution fusion | flops 1258291200 | bytes 7471104 | tf_op jit(solution)/shard_map/dot_general | solution.py:88
  101.0 2.8 %convolution_add_fusion.6 = f32[2048,320]{0,1:T(8,128)S(1)} fusion(f32[2048,320]{0,1:T(8,128)S(1)} %fusion.30, bf16[2048,960]{1,0:T(8,128)(2,1)S(1)} %bitcast.84, bf16[3,3,960,320]{2,3,1,0:T(8,128)(2,1)} %param.19), kind=kOutput, calls=%fused_computation.32 | convolution fusion | flops 1258946560 | bytes 9830400 | tf_op jit(solution)/shard_map/dot_general | solution.py:88
  103.9 0.2 slice-done.1
  104.0 1.6 %convolution_add_fusion.5 = f32[2048,320]{0,1:T(8,128)S(1)} fusion(f32[2048,320]{0,1:T(8,128)S(1)} %convolution_add_fusion.6, bf16[2048,960]{1,0:T(8,128)(2,1)S(1)} %bitcast.83, bf16[3,3,960,320]{2,3,1,0:T(8,128)(2,1)S(1)} %bitcast.90), kind=kOutput, calls=%fused_computation.31 | convolution fusion | flops 1258946560 | bytes 10092544 | tf_op jit(solution)/shard_map/dot_general | solution.py:88
  105.6 0.6 copy-done.3
  106.2 1.6 %convolution_add_fusion.4 = f32[2048,320]{0,1:T(8,128)S(1)} fusion(f32[2048,320]{0,1:T(8,128)S(1)} %convolution_add_fusion.5, bf16[2048,960]{1,0:T(8,128)(2,1)S(1)} %bitcast.82, bf16[3,3,960,320]{2,3,1,0:T(8,128)(2,1)S(1)} %bitcast.90), kind=kOutput, calls=%fused_computation.30 | convolution fusion | flops 1258946560 | bytes 10092544 | tf_op jit(solution)/shard_map/dot_general | solution.py:88
  107.8 0.6 copy-done.7
  108.4 3.1 %fusion.24 = f32[2048,320]{0,1:T(8,128)} fusion(bf16[2048,960]{1,0:T(8,128)(2,1)S(1)} %bitcast.87, bf16[3,3,960,320]{2,3,1,0:T(8,128)(2,1)S(1)} %bitcast.90), kind=kOutput, calls=%fused_computation.45 | convolution fusion | flops 1258291200 | bytes 7471104 | tf_op jit(solution)/shard_map/dot_general | solution.py:88
  111.5 3.5 %fusion.12 = f32[2048,320]{0,1:T(8,128)S(1)} fusion(f32[2048,320]{0,1:T(8,128)} %fusion.24, f32[2048,320]{0,1:T(8,128)S(1)} %convolution_add_fusion.4, bf16[2048,960]{1,0:T(8,128)(2,1)S(1)} %bitcast.85, bf16[3,3,960,320]{2,3,1,0:T(8,128)(2,1)S(1)} %bitcast.90), kind=kOutput, calls=%fused_computation.26 | convolution fusion | flops 1259601920 | bytes 12713984 | tf_op jit(solution)/shard_map/dot_general | solution.py:88
  115.0 1.6 %convolution_add_fusion.3 = f32[2048,320]{0,1:T(8,128)S(1)} fusion(f32[2048,320]{0,1:T(8,128)S(1)} %fusion.12, bf16[2048,960]{1,0:T(8,128)(2,1)S(1)} %bitcast.81, bf16[3,3,960,320]{2,3,1,0:T(8,128)(2,1)S(1)} %bitcast.90), kind=kOutput, calls=%fused_computation.29 | convolution fusion | flops 1258946560 | bytes 10092544 | tf_op jit(solution)/shard_map/dot_general | solution.py:88
  116.6 1.6 %convolution_add_fusion.2 = f32[2048,320]{0,1:T(8,128)S(1)} fusion(f32[2048,320]{0,1:T(8,128)S(1)} %convolution_add_fusion.3, bf16[2048,960]{1,0:T(8,128)(2,1)S(1)} %bitcast.80, bf16[3,3,960,320]{2,3,1,0:T(8,128)(2,1)S(1)} %bitcast.90), kind=kOutput, calls=%fused_computation.28 | convolution fusion | flops 1258946560 | bytes 10092544 | tf_op jit(solution)/shard_map/dot_general | solution.py:88
  118.3 1.9 %convolution_add_fusion.1 = f32[2048,320]{0,1:T(8,128)S(1)} fusion(f32[2048,320]{0,1:T(8,128)S(1)} %convolution_add_fusion.2, bf16[2048,960]{1,0:T(8,128)(2,1)S(1)} %bitcast.79, bf16[3,3,960,320]{2,3,1,0:T(8,128)(2,1)S(1)} %bitcast.90), kind=kOutput, calls=%fused_computation.27 | convolution fusion | flops 1258946560 | bytes 10092544 | tf_op jit(solution)/shard_map/dot_general | solution.py:88
  120.2 3.3 %fusion.9 = f32[2048,320]{0,1:T(8,128)} fusion(f32[2048,320]{0,1:T(8,128)S(1)} %convolution_add_fusion.1, bf16[960,320]{0,1:T(8,128)(2,1)S(1)} %copy-done.14, bf16[2048,640]{1,0:T(8,128)(2,1)S(1)} %bitcast.76, bf16[2048,320]{1,0:T(8,128)(2,1)S(1)} %bitcast.78), kind=kOutput, calls=%fused_computation.24 | convolution fusion | flops 1266810880 | bytes 9789440 | tf_op jit(solution)/shard_map/dot_general | solution.py:91
  123.5 2.9 %fusion.17 = bf16[2,64,960]{2,0,1:T(2,128)(2,1)S(1)} fusion(bf16[16,64,960]{2,1,0:T(8,128)(2,1)} %all-gather.2.cloned.1.call-done, s32[16]{0:T(128)S(1)} %all-reduce.1, s32[2]{0:T(128)S(1)} %copy-done.13), kind=kOutput, calls=%fused_computation.39 | convolution fusion | flops 4055072 | bytes 2211912 | tf_op jit(solution)/shard_map/rk,kij->rij/dot_general | solution.py:72
  126.4 6.0 %fusion.14 = bf16[2,1024,320]{1,2,0:T(8,128)(2,1)} fusion(f32[40,2,8,1024]{3,2,1,0:T(8,128)} %bitcast.91, f32[320]{0:T(512)S(1)} %copy-done.12, bf16[2,1024,960]{2,1,0:T(8,128)(2,1)} %multiply_convert_fusion, bf16[2,64,960]{2,0,1:T(2,128)(2,1)S(1)} %fusion.17, bf16[2,64,320]{2,0,1:T(2,128)(2,1)S(1)} %convolution_convert_fusion.1), kind=kOutput, calls=%fused_computation.35 | convolution fusion | flops 337641472 | bytes 8193280 | tf_op jit(solution)/shard_map/rpk,rko->rpo/dot_general | solution.py:99
  (48 shorter events, 0.2 us)
Async XLA Ops:
  6.5 1.8 %copy-start = (bf16[16,128,640]{2,1,0:T(8,128)(2,1)S(1)}, bf16[16,128,640]{2,1,0:T(8,128)(2,1)}, u32[]{:S(2)}) copy-start(bf16[16,128,640]{2,1,0:T(8,128)(2,1)} %param.13) | copy-start | bytes 7864324
  10.7 9.0 %copy-start.9 = (bf16[4,64,320]{2,1,0:T(8,128)(2,1)S(1)}, bf16[4,64,320]{2,1,0:T(8,128)(2,1)}, u32[]{:S(2)}) copy-start(bf16[4,64,320]{2,1,0:T(8,128)(2,1)} %param.18) | copy-start | bytes 491524
  14.3 23.8 %copy-start.8 = (bf16[2,1024,320]{1,2,0:T(8,128)(2,1)S(1)}, bf16[2,1024,320]{1,2,0:T(8,128)(2,1)}, u32[]{:S(2)}) copy-start(bf16[2,1024,320]{1,2,0:T(8,128)(2,1)} %param.12) | copy-start | bytes 3932164
  14.3 25.4 %copy-start.16 = (u32[32]{0:T(128)S(1)}, u32[32]{0:T(128)}, u32[]{:S(2)}) copy-start(u32[32]{0:T(128)} %constant.55) | copy-start | bytes 388
  14.3 26.6 %copy-start.15 = (s32[4]{0:T(128)S(1)}, s32[4]{0:T(128)}, u32[]{:S(2)}) copy-start(s32[4]{0:T(128)} %param.16) | copy-start | bytes 52
  14.3 37.7 %all-to-all-start = ((bf16[2,8,128,640]{3,2,0,1:T(8,128)(2,1)}), bf16[2,8,128,640]{3,2,0,1:T(8,128)(2,1)}, u32[]{:S(2)}, u32[]{:S(2)}) async-start(bf16[2,8,128,640]{3,2,0,1:T(8,128)(2,1)} %copy.36), calls=%async_computation | async-start | bytes 5242880 | tf_op jit(solution)/shard_map/all_to_all | solution.py:66
  19.6 31.8 %copy-start.13 = (s32[2]{0:T(128)S(1)}, s32[2]{0:T(128)}, u32[]{:S(2)}) copy-start(s32[2]{0:T(128)} %param.15) | copy-start | bytes 28
  19.6 103.8 %all-gather.2.cloned.1.call-start = ((), (), s32[]{:S(2)}) async-start(), calls=%async_computation.1 | async-start | bytes 2621440 | tf_op jit(solution)/shard_map/all_gather | solution.py:68
  19.8 9.7 %collective-permute-start = (bf16[4,64,320]{2,0,1:T(4,128)(2,1)S(1)}, bf16[4,64,320]{2,0,1:T(4,128)(2,1)S(1)}, u32[]{:S(2)}, u32[]{:S(2)}) collective-permute-start(bf16[4,64,320]{2,0,1:T(4,128)(2,1)S(1)} %copy.48), channel_id=1, source_target_pairs={{0,1},{1,2},{2,3},{3,0},{4,5},{5,6},{6,7},{7,4},{8,9},{9,10},{10,1... | collective-permute-start | bytes 491528 | tf_op jit(solution)/shard_map/ppermute | solution.py:19
  29.6 8.4 %collective-permute-start.1 = (bf16[4,64,320]{2,0,1:T(4,128)(2,1)S(1)}, bf16[4,64,320]{2,0,1:T(4,128)(2,1)S(1)}, u32[]{:S(2)}, u32[]{:S(2)}) collective-permute-start(bf16[4,64,320]{2,0,1:T(4,128)(2,1)S(1)} %collective-permute-done), channel_id=1, source_target_pairs={{0,1},{1,2},{2,3},{3,0},{4,5},{5,6},{6,7},{7,4},{8,9},{9,10},{10,1... | collective-permute-start | bytes 491528 | tf_op jit(solution)/shard_map/ppermute | solution.py:19
  38.0 11.4 %collective-permute-start.2 = (bf16[4,64,320]{2,0,1:T(4,128)(2,1)S(1)}, bf16[4,64,320]{2,0,1:T(4,128)(2,1)S(1)}, u32[]{:S(2)}, u32[]{:S(2)}) collective-permute-start(bf16[4,64,320]{2,0,1:T(4,128)(2,1)S(1)} %collective-permute-done.1), channel_id=1, source_target_pairs={{0,1},{1,2},{2,3},{3,0},{4,5},{5,6},{6,7},{7,4},{8,9},{9,10},{10,1... | collective-permute-start | bytes 491528 | tf_op jit(solution)/shard_map/ppermute | solution.py:19
  54.1 7.8 %copy-start.10 = (f32[960]{0:T(1024)S(1)}, f32[960]{0:T(1024)}, u32[]{:S(2)}) copy-start(f32[960]{0:T(1024)} %param.22) | copy-start | bytes 11524
  54.1 7.8 %copy-start.11 = (f32[960]{0:T(1024)S(1)}, f32[960]{0:T(1024)}, u32[]{:S(2)}) copy-start(f32[960]{0:T(1024)} %param.21) | copy-start | bytes 11524
  61.9 6.9 %copy-start.2 = (bf16[2,1024,320]{2,1,0:T(8,128)(2,1)S(1)}, bf16[2,1024,320]{2,1,0:T(8,128)(2,1)}, u32[]{:S(2)}) copy-start(bf16[2,1024,320]{2,1,0:T(8,128)(2,1)} %copy.53) | copy-start | bytes 3932164
  96.9 4.1 %copy-start.5 = (bf16[2,32,32,960]{3,2,1,0:T(8,128)(2,1)S(1)}, bf16[2,32,32,960]{3,2,1,0:T(8,128)(2,1)}, u32[]{:S(2)}) copy-start(bf16[2,32,32,960]{3,2,1,0:T(8,128)(2,1)} %get-tuple-element.6) | copy-start | bytes 11796484
  96.9 6.9 %slice-start = ((s8[5898240]{0:T(1024)(128)(4,1)}), s8[4194304]{0:T(1024)(128)(4,1)S(1)}, s32[]{:S(2)}) async-start(s8[5898240]{0:T(1024)(128)(4,1)} %bitcast.89), calls=%async_computation.2 | async-start | bytes 8388608
  101.0 2.9 %copy-start.4 = (bf16[2,32,32,960]{3,2,1,0:T(8,128)(2,1)S(1)}, bf16[2,32,32,960]{3,2,1,0:T(8,128)(2,1)}, u32[]{:S(2)}) copy-start(bf16[2,32,32,960]{3,2,1,0:T(8,128)(2,1)} %get-tuple-element.7) | copy-start | bytes 11796484
  101.0 3.0 %slice-start.1 = ((s8[5898240]{0:T(1024)(128)(4,1)}), s8[1703936]{0:T(1024)(128)(4,1)S(1)}, s32[]{:S(2)}) async-start(s8[5898240]{0:T(1024)(128)(4,1)} %bitcast.89), calls=%async_computation.3 | async-start | bytes 3407872
  104.0 2.2 %copy-start.3 = (bf16[2,32,32,960]{3,2,1,0:T(8,128)(2,1)S(1)}, bf16[2,32,32,960]{3,2,1,0:T(8,128)(2,1)}, u32[]{:S(2)}) copy-start(bf16[2,32,32,960]{3,2,1,0:T(8,128)(2,1)} %get-tuple-element.8) | copy-start | bytes 11796484
  106.2 2.2 %copy-start.7 = (bf16[2,32,32,960]{3,2,1,0:T(8,128)(2,1)S(1)}, bf16[2,32,32,960]{3,2,1,0:T(8,128)(2,1)}, u32[]{:S(2)}) copy-start(bf16[2,32,32,960]{3,2,1,0:T(8,128)(2,1)} %get-tuple-element.9) | copy-start | bytes 11796484
  108.4 3.1 %copy-start.6 = (bf16[2,1024,960]{2,1,0:T(8,128)(2,1)S(1)}, bf16[2,1024,960]{2,1,0:T(8,128)(2,1)}, u32[]{:S(2)}) copy-start(bf16[2,1024,960]{2,1,0:T(8,128)(2,1)} %multiply_convert_fusion) | copy-start | bytes 11796484
  118.3 1.9 %copy-start.14 = (bf16[960,320]{0,1:T(8,128)(2,1)S(1)}, bf16[960,320]{0,1:T(8,128)(2,1)}, u32[]{:S(2)}) copy-start(bf16[960,320]{0,1:T(8,128)(2,1)} %param.20) | copy-start | bytes 1843204
  120.2 6.2 %copy-start.12 = (f32[320]{0:T(512)S(1)}, f32[320]{0:T(512)}, u32[]{:S(2)}) copy-start(f32[320]{0:T(512)} %param.23) | copy-start | bytes 3844
  126.4 6.0 %copy-start.1 = (bf16[16,128,640]{2,1,0:T(8,128)(2,1)S(1)}, bf16[16,128,640]{2,1,0:T(8,128)(2,1)}, u32[]{:S(2)}) copy-start(bf16[16,128,640]{2,1,0:T(8,128)(2,1)} %param.13) | copy-start | bytes 7864324
Sparse Core Ops, SparseCore 0:
  38.2 47.3 all-gather.1
